TPU v7x, 32 devices: a whole 2x2x4 slice. The times are simulated.
32 devices in a mesh: node: 8 (over z, x), local: 4 (over y, core).
Axes of the slice: x: 2, y: 2, z: 4, core: 2. Of those that a mesh axis runs over, the one named last changes fastest.
Arguments:
- tokens: bfloat16 [512, 7168], P(('node', 'local')), may hold values from -6 to 6
- out_grads: bfloat16 [512, 7168], P(('node', 'local')), may hold values from -0.59765625 to 0.59765625
- routes: int32 [512, 8], P(('node', 'local')), may hold values from 0 to 15, as said below
- gate_values: float32 [512, 8], P(('node', 'local')), may hold values from 0.1 to 1
- gate_weight: bfloat16 [32, 7168, 512], P(('node', 'local')), may hold values from -0.0625 to 0.0625
- up_weight: bfloat16 [32, 7168, 512], P(('node', 'local')), may hold values from -0.0625 to 0.0625
- down_weight: bfloat16 [32, 512, 7168], P(('node', 'local')), may hold values from -0.1875 to 0.1875
Outputs:
- input_grads: bfloat16 [512, 7168], P(('node', 'local'))
- gate_grads: float32 [512, 8], P(('node', 'local'))
Inputs may be any that keep to these rules, and one draw needn't show every extreme that they name: `routes`: each row names 8 different experts, 2 from each of 4 different groups (group of e is e // 2). Among the 16 rows of one device, at most 13 rows use a given group and at most 13 rows name a given expert; in every draw some group and some expert reach these bounds from every device.
All inputs are finite; a program needn't handle non-finite values.
Results may differ from a plain program's by a relative error of at most 0.012.
Values may be sent and summed in bfloat16 or wider, within the bound.
A program may use at most 128 MiB of HBM per device.

v0:
```python
import jax
import jax.numpy as jnp
from jax import lax
from jax.sharding import PartitionSpec as P

NODE_LIMIT = 4
PER_NODE = 2


def shard_terms(rows_x, rows_dy, w_gate, w_up, w_down):
    pre_gate = jnp.dot(rows_x, w_gate, preferred_element_type=jnp.float32)
    pre_up = jnp.dot(rows_x, w_up, preferred_element_type=jnp.float32)
    sigmoid_gate = jax.nn.sigmoid(pre_gate)
    activated = pre_gate * sigmoid_gate
    hidden = (activated * pre_up).astype(jnp.bfloat16)
    back_grad = lax.dot_general(
        rows_dy, w_down, (((1,), (1,)), ((), ())), preferred_element_type=jnp.float32
    )
    part_gate = jnp.sum(hidden.astype(jnp.float32) * back_grad, axis=1)
    d_gate = (back_grad * pre_up * sigmoid_gate * (1.0 + pre_gate * (1.0 - sigmoid_gate))).astype(
        jnp.bfloat16
    )
    d_up = (back_grad * activated).astype(jnp.bfloat16)
    part_dx = lax.dot_general(
        d_gate, w_gate, (((1,), (1,)), ((), ())), preferred_element_type=jnp.float32
    )
    part_dx = part_dx + lax.dot_general(
        d_up, w_up, (((1,), (1,)), ((), ())), preferred_element_type=jnp.float32
    )
    gate_high = part_gate.astype(jnp.bfloat16)
    gate_low = (part_gate - gate_high.astype(jnp.float32)).astype(jnp.bfloat16)
    return (part_dx.astype(jnp.bfloat16), jnp.stack([gate_high, gate_low], axis=-1))


def finish_slots(
    backward_input_gradient, back_gate, position, gate_values, slots, width, row_count, pick_count
):
    flat_index = position.reshape(-1)
    picked = jnp.take(backward_input_gradient.reshape(slots, width), flat_index, axis=0).reshape(
        row_count, pick_count, 2, width
    )
    weighted = jnp.sum(picked.astype(jnp.float32) * gate_values[:, :, None, None], axis=(1, 2))
    gate_parts = jnp.take(back_gate.reshape(slots, 2), flat_index, axis=0).astype(jnp.float32)
    gate_grads = jnp.sum(gate_parts.reshape(row_count, pick_count, 4), axis=2)
    return (weighted.astype(jnp.bfloat16), gate_grads)


def on_device(tokens, out_grads, routes, gate_values, gate_weight, up_weight, down_weight):
    n_node = lax.axis_size("node")
    n_local = lax.axis_size("local")
    devices = n_node * n_local
    row_count = tokens.shape[0]
    pick_count = routes.shape[1]
    width = tokens.shape[1]
    exp_node = n_local // 2
    experts = devices // 2
    node_capacity_limit = min(
        row_count, NODE_LIMIT * (row_count - 1) // (n_node - NODE_LIMIT + 1) + 1
    )
    cap_exp = min(
        node_capacity_limit, PER_NODE * (node_capacity_limit - 1) // (exp_node - PER_NODE + 1) + 1
    )
    w_gate = gate_weight[0]
    w_up = up_weight[0]
    w_down = down_weight[0]
    token_ids = jnp.arange(row_count, dtype=jnp.int32)
    half_ids = jnp.arange(2, dtype=jnp.int32)
    pick_ids = jnp.arange(pick_count, dtype=jnp.int32)
    expert_hot = routes[:, :, None] == jnp.arange(experts, dtype=jnp.int32)[None, None, :]
    per_expert = jnp.any(expert_hot, axis=1).astype(jnp.int32)
    expert_before = jnp.cumsum(per_expert, axis=0) - per_expert
    rank_e = jnp.sum(jnp.where(expert_hot, expert_before[:, None, :], 0), axis=2)
    dest_dev = 2 * routes[:, :, None] + half_ids[None, None, :]
    slots = devices * cap_exp
    node_of = routes // exp_node
    node_hot = node_of[:, :, None] == jnp.arange(n_node, dtype=jnp.int32)[None, None, :]
    per_node = jnp.any(node_hot, axis=1).astype(jnp.int32)
    node_before = jnp.cumsum(per_node, axis=0) - per_node
    node_rank = jnp.sum(jnp.where(node_hot, node_before[:, None, :], 0), axis=2)
    slot_one = (node_of * node_capacity_limit + node_rank).reshape(-1)
    same_before = (node_of[:, :, None] == node_of[:, None, :]) & (
        pick_ids[None, None, :] < pick_ids[None, :, None]
    )
    pick_slot = jnp.sum(same_before.astype(jnp.int32), axis=2).reshape(-1)
    slot_code = (1 + routes % exp_node * cap_exp + rank_e).reshape(-1)
    rows_one = n_node * node_capacity_limit
    owner_ids = jnp.broadcast_to(token_ids[:, None], routes.shape).reshape(-1)
    source_one = (
        jnp.full((rows_one,), row_count, jnp.int32).at[slot_one].set(owner_ids, mode="drop")
    )
    slot_codes = (
        jnp.zeros((rows_one, PER_NODE), jnp.float32)
        .at[slot_one, pick_slot]
        .set(slot_code.astype(jnp.float32), mode="drop")
    )
    slot_codes = slot_codes.astype(jnp.bfloat16).reshape(n_node, node_capacity_limit, PER_NODE)
    send_x = jnp.take(tokens, source_one, axis=0, mode="fill", fill_value=0).reshape(
        n_node, node_capacity_limit, width
    )
    send_dy = jnp.take(out_grads, source_one, axis=0, mode="fill", fill_value=0).reshape(
        n_node, node_capacity_limit, width
    )
    mid_x, mid_dy, mid_payload = (
        lax.all_to_all(send_x, "node", split_axis=0, concat_axis=0, tiled=True),
        lax.all_to_all(send_dy, "node", split_axis=0, concat_axis=0, tiled=True),
        lax.all_to_all(slot_codes, "node", split_axis=0, concat_axis=0, tiled=True),
    )
    mid_payload = mid_payload.reshape(rows_one, -1)
    code_int = mid_payload.astype(jnp.int32)
    is_live = code_int > 0
    local_pick = (code_int - 1) // cap_exp
    slot_rank = (code_int - 1) % cap_exp
    anchor = jnp.arange(rows_one, dtype=jnp.int32) // node_capacity_limit
    dest_two = (
        (2 * local_pick[:, :, None] + half_ids[None, None, :]) * n_node + anchor[:, None, None]
    ) * cap_exp + slot_rank[:, :, None]
    dest_two = jnp.where(is_live[:, :, None], dest_two, slots)
    mid_ids = jnp.broadcast_to(
        jnp.arange(rows_one, dtype=jnp.int32)[:, None, None], dest_two.shape
    ).reshape(-1)
    source_two = (
        jnp.full((slots,), rows_one, jnp.int32).at[dest_two.reshape(-1)].set(mid_ids, mode="drop")
    )
    out_x = jnp.take(mid_x.reshape(rows_one, width), source_two, axis=0, mode="fill", fill_value=0)
    out_dy = jnp.take(
        mid_dy.reshape(rows_one, width), source_two, axis=0, mode="fill", fill_value=0
    )
    got_x, got_dy = (
        lax.all_to_all(
            out_x.reshape(n_local, n_node * cap_exp, width),
            "local",
            split_axis=0,
            concat_axis=0,
            tiled=True,
        ),
        lax.all_to_all(
            out_dy.reshape(n_local, n_node * cap_exp, width),
            "local",
            split_axis=0,
            concat_axis=0,
            tiled=True,
        ),
    )
    part_dx, gate_pair = shard_terms(
        got_x.reshape(slots, width), got_dy.reshape(slots, width), w_gate, w_up, w_down
    )
    backward_input_gradient, back_gate = (
        lax.all_to_all(
            lax.all_to_all(
                part_dx.reshape(n_local, n_node, cap_exp, width),
                "node",
                split_axis=1,
                concat_axis=1,
                tiled=True,
            ),
            "local",
            split_axis=0,
            concat_axis=0,
            tiled=True,
        ),
        lax.all_to_all(
            lax.all_to_all(
                gate_pair.reshape(n_local, n_node, cap_exp, 2),
                "node",
                split_axis=1,
                concat_axis=1,
                tiled=True,
            ),
            "local",
            split_axis=0,
            concat_axis=0,
            tiled=True,
        ),
    )
    position = (dest_dev % n_local * n_node + dest_dev // n_local) * cap_exp + rank_e[:, :, None]
    return finish_slots(
        backward_input_gradient,
        back_gate,
        position,
        gate_values,
        slots,
        width,
        row_count,
        pick_count,
    )


def solution(mesh):
    in_specs = (
        P(("node", "local"), None),
        P(("node", "local"), None),
        P(("node", "local"), None),
        P(("node", "local"), None),
        P(("node", "local"), None, None),
        P(("node", "local"), None, None),
        P(("node", "local"), None, None),
    )
    out_specs = (P(("node", "local"), None), P(("node", "local"), None))
    return jax.shard_map(
        on_device, mesh=mesh, in_specs=in_specs, out_specs=out_specs, check_vma=False
    )
```

profile of v0, /device:TPU:0, one launch (start us, length us, event | category | flops | bytes accessed | tf_op | source)
XLA Modules:
  0.0 607.8 jit_solution(2878147194063423985)
XLA Ops:
  3.5 6.4 %scatter_fusion = f32[104,2]{0,1:T(2,128)S(1)} fusion(f32[104,2]{0,1:T(2,128)S(1)} %broadcast_in_dim.128, s32[128]{0:T(128)S(1)} %get-tuple-element.29, f32[128]{0:T(128)S(1)} %reshape.541), kind=kCustom, calls=%fused_computation.7 | custom fusion | bytes 2560 | tf_op jit(solution)/shard_map/scatter | solution.py:94
  10.6 7.3 %all-to-all-start.1 = ((bf16[8,13,2]{1,2,0:T(2,128)(2,1)}), bf16[8,13,2]{1,2,0:T(2,128)(2,1)S(1)}, u32[]{:S(2)}, u32[]{:S(2)}) async-start(bf16[8,13,2]{1,2,0:T(2,128)(2,1)} %copy.122), calls=%async_computation.1 | async-start | bytes 8192 | tf_op jit(solution)/shard_map/all_to_all | solution.py:106
  36.5 40.2 %all-to-all-done.3 = bf16[8,13,7168]{2,1,0:T(8,128)(2,1)S(1)} async-done(((bf16[8,13,7168]{2,1,0:T(8,128)(2,1)}), bf16[8,13,7168]{2,1,0:T(8,128)(2,1)S(1)}, u32[]{:S(2)}, u32[]{:S(2)}) %all-to-all-start.3) | async-done | bytes 1490976 | tf_op jit(solution)/shard_map/all_to_all | solution.py:104
  87.1 6.6 %gather_fusion.5 = bf16[416,7168]{1,0:T(8,128)(2,1)} fusion(bf16[104,7168]{1,0:T(8,128)(2,1)S(1)} %reshape.474, s32[1024]{0:T(1024)S(1)} %pad_clamp_fusion.1), kind=kCustom, calls=%fused_computation.3.clone | custom fusion | bytes 11929216 | tf_op jit(solution)/shard_map/jit(_take)/gather | solution.py:124
  93.7 29.6 %all-to-all-done = bf16[8,13,7168]{2,1,0:T(8,128)(2,1)} async-done(((bf16[8,13,7168]{2,1,0:T(8,128)(2,1)}), bf16[8,13,7168]{2,1,0:T(8,128)(2,1)}, u32[]{:S(2)}, u32[]{:S(2)}) %all-to-all-start) | async-done | bytes 1490976 | tf_op jit(solution)/shard_map/all_to_all | solution.py:105
  125.4 6.6 %gather_fusion.3 = bf16[416,7168]{1,0:T(8,128)(2,1)} fusion(bf16[104,7168]{1,0:T(8,128)(2,1)S(1)} %reshape.467, s32[1024]{0:T(1024)S(1)} %pad_clamp_fusion.1), kind=kCustom, calls=%fused_computation.1.clone | custom fusion | bytes 11929216 | tf_op jit(solution)/shard_map/jit(_take)/gather | solution.py:125
  132.0 9.7 %broadcast_select_fusion.2 = (bf16[416,7168]{1,0:T(8,128)(2,1)}, bf16[416,7168]{1,0:T(8,128)(2,1)}) fusion(bf16[416,7168]{1,0:T(8,128)(2,1)} %gather_fusion.3, pred[416]{0:T(512)(128)(4,1)S(1)} %compare_and_fusion.1, bf16[416,7168]{1,0:T(8,128)(2,1)} %gather_fusion.5), kind=kLoop, calls=%fused_computation.22 | loop fusion | flops 5963776 | bytes 23855520 | tf_op jit(solution)/shard_map/jit(_take)/select_n | solution.py:125
  141.7 73.8 %all_to_all.45 = bf16[4,104,7168]{2,1,0:T(8,128)(2,1)} all-to-all(bf16[4,104,7168]{2,1,0:T(8,128)(2,1)} %bitcast.43), channel_id=1, replica_groups=mesh['node'=8,'local'=4] {'local'}, dimensions={0} | all-to-all | bytes 11927552 | tf_op jit(solution)/shard_map/all_to_all | solution.py:129
  221.1 9.2 %fusion.2 = f32[416,512]{1,0:T(8,128)} fusion(bf16[416,7168]{1,0:T(8,128)(2,1)} %bitcast.46, bf16[1,7168,512]{2,1,0:T(8,128)(2,1)} %param.15), kind=kOutput, calls=%fused_computation.12 | convolution fusion | flops 3053453312 | bytes 14155776 | tf_op jit(solution)/shard_map/dot_general | solution.py:11
  234.5 53.8 %all-to-all-done.2 = bf16[4,104,7168]{2,1,0:T(8,128)(2,1)} async-done(((bf16[4,104,7168]{2,1,0:T(8,128)(2,1)}), bf16[4,104,7168]{2,1,0:T(8,128)(2,1)}, u32[]{:S(2)}, u32[]{:S(2)}) %all-to-all-start.2) | async-done | bytes 5963808 | tf_op jit(solution)/shard_map/all_to_all | solution.py:136
  288.3 8.8 %multiply_reduce_fusion.1 = (f32[416]{0:T(512)S(1)}, f32[416,512]{1,0:T(8,128)S(1)}) fusion(f32[416,512]{1,0:T(8,128)} %fusion.5, f32[416,512]{1,0:T(8,128)} %fusion.2, bf16[416,7168]{1,0:T(8,128)(2,1)} %bitcast.4, bf16[1,512,7168]{2,1,0:T(8,128)(2,1)} %param.17), kind=kOutput, calls=%fused_computation.25 | convolution fusion | flops 3055369728 | bytes 15861376 | tf_op jit(solution)/shard_map/dot_general | solution.py:16
  297.0 10.5 %fusion = f32[416,7168]{1,0:T(8,128)} fusion(bf16[1,7168,512]{2,1,0:T(8,128)(2,1)} %param.15, f32[416,512]{1,0:T(8,128)S(1)} %copy-done.4, f32[416,512]{1,0:T(8,128)S(1)} %get-tuple-element.32, f32[416,512]{1,0:T(8,128)S(1)} %copy-done.5), kind=kOutput, calls=%fused_computation.10 | convolution fusion | flops 3055583232 | bytes 21823488 | tf_op jit(solution)/shard_map/dot_general | solution.py:24
  312.2 11.3 %add_convert_fusion = bf16[416,7168]{1,0:T(8,128)(2,1)} fusion(f32[416,7168]{1,0:T(8,128)} %fusion, bf16[1,7168,512]{2,1,0:T(8,128)(2,1)} %param.16, f32[416,512]{1,0:T(8,128)S(1)} %get-tuple-element.32, f32[416,512]{1,0:T(8,128)S(1)} %copy-done.4), kind=kOutput, calls=%fused_computation.9 | convolution fusion | flops 3060695040 | bytes 26935296 | tf_op jit(solution)/shard_map/dot_general | solution.py:27
  323.5 7.0 %reshape.477 = bf16[4,8,13,7168]{3,2,1,0:T(8,128)(2,1)} reshape(bf16[416,7168]{1,0:T(8,128)(2,1)} %add_convert_fusion) | data formatting | bytes 11927552 | tf_op jit(solution)/shard_map/reshape | solution.py:150
  330.5 10.5 %copy.127 = bf16[4,8,13,7168]{3,0,2,1:T(4,128)(2,1)} copy(bf16[4,8,13,7168]{3,2,1,0:T(8,128)(2,1)} %reshape.477) | data formatting | bytes 11927552 | tf_op jit(solution)/shard_map/reshape | solution.py:150
  341.0 6.0 all-to-all-start.5
  347.6 129.8 %all-to-all-done.5 = bf16[4,8,13,7168]{3,0,2,1:T(4,128)(2,1)} async-done(((bf16[4,8,13,7168]{3,0,2,1:T(4,128)(2,1)}), bf16[4,8,13,7168]{3,0,2,1:T(4,128)(2,1)}, u32[]{:S(2)}, u32[]{:S(2)}) %all-to-all-start.5) | async-done | bytes 5963808 | tf_op jit(solution)/shard_map/all_to_all | solution.py:149
  480.7 7.0 %copy.128 = bf16[4,8,13,7168]{3,1,2,0:T(8,128)(2,1)} copy(bf16[4,8,13,7168]{3,0,2,1:T(4,128)(2,1)} %all-to-all-done.5) | data formatting | bytes 11927552 | tf_op jit(solution)/shard_map/all_to_all | solution.py:149
  496.9 63.6 %all-to-all-done.6 = bf16[4,8,13,7168]{3,1,2,0:T(8,128)(2,1)} async-done(((bf16[4,8,13,7168]{3,1,2,0:T(8,128)(2,1)}), bf16[4,8,13,7168]{3,1,2,0:T(8,128)(2,1)}, u32[]{:S(2)}, u32[]{:S(2)}) %all-to-all-start.6) | async-done | bytes 5963808 | tf_op jit(solution)/shard_map/all_to_all | solution.py:148
  560.5 9.0 %copy.129 = bf16[4,8,13,7168]{3,2,1,0:T(8,128)(2,1)} copy(bf16[4,8,13,7168]{3,1,2,0:T(8,128)(2,1)} %all-to-all-done.6) | data formatting | bytes 11927552 | tf_op jit(solution)/shard_map/all_to_all | solution.py:148
  569.5 7.5 %reshape.478 = bf16[416,7168]{1,0:T(8,128)(2,1)} reshape(bf16[4,8,13,7168]{3,2,1,0:T(8,128)(2,1)} %copy.129) | data formatting | bytes 11927552 | tf_op jit(solution)/shard_map/reshape | solution.py:39
  577.0 11.5 %gather_fusion = bf16[256,7168]{1,0:T(8,128)(2,1)} fusion(bf16[416,7168]{1,0:T(8,128)(2,1)} %reshape.478, s32[1024]{0:T(1024)S(1)} %pad_clamp_fusion), kind=kCustom, calls=%fused_computation.4 | custom fusion | bytes 7341056 | tf_op jit(solution)/shard_map/jit(_take)/gather | solution.py:39
  588.5 8.3 %gather.17 = bf16[16,8,2,7168]{3,2,1,0:T(2,128)(2,1)} reshape(bf16[256,7168]{1,0:T(8,128)(2,1)} %gather_fusion) | data formatting | bytes 7340032 | tf_op jit(solution)/shard_map/jit(_take)/gather | solution.py:39
  596.8 10.8 %multiply_reduce_fusion = bf16[16,7168]{1,0:T(8,128)(2,1)} fusion(bf16[16,8,2,7168]{3,2,1,0:T(2,128)(2,1)} %gather.17, pred[16,8,2]{2,1,0:T(8,128)(4,1)S(1)} %copy.111, f32[16,8]{1,0:T(8,128)S(1)} %copy.132), kind=kLoop, calls=%fused_computation.19 | loop fusion | flops 7225344 | bytes 3900160 | tf_op jit(solution)/shard_map/reduce_sum | solution.py:42
  (127 shorter events, 61.9 us)
Async XLA Ops:
  0.6 18.3 %copy-start = (bf16[16,7168]{1,0:T(8,128)(2,1)S(1)}, bf16[16,7168]{1,0:T(8,128)(2,1)}, u32[]{:S(2)}) copy-start(bf16[16,7168]{1,0:T(8,128)(2,1)} %param.12) | copy-start | bytes 688132
  2.5 0.6 copy-start.6
  10.6 17.5 %all-to-all-start.1 = ((bf16[8,13,2]{1,2,0:T(2,128)(2,1)}), bf16[8,13,2]{1,2,0:T(2,128)(2,1)S(1)}, u32[]{:S(2)}, u32[]{:S(2)}) async-start(bf16[8,13,2]{1,2,0:T(2,128)(2,1)} %copy.122), calls=%async_computation.1 | async-start | bytes 8192 | tf_op jit(solution)/shard_map/all_to_all | solution.py:106
  18.9 2.6 copy-start.2
  28.1 0.6 copy-start.8
  28.7 48.1 %all-to-all-start.3 = ((bf16[8,13,7168]{2,1,0:T(8,128)(2,1)}), bf16[8,13,7168]{2,1,0:T(8,128)(2,1)S(1)}, u32[]{:S(2)}, u32[]{:S(2)}) async-start(bf16[8,13,7168]{2,1,0:T(8,128)(2,1)} %reshape.473), calls=%async_computation.3 | async-start | bytes 3670016 | tf_op jit(solution)/shard_map/all_to_all | solution.py:104
  34.7 46.6 %copy-start.9 = (bf16[8,13,2]{1,2,0:T(2,128)(2,1)S(1)}, bf16[8,13,2]{1,2,0:T(2,128)(2,1)}, u32[]{:S(2)}) copy-start(bf16[8,13,2]{1,2,0:T(2,128)(2,1)} %copy-done.8) | copy-start | bytes 1252
  76.8 46.6 %all-to-all-start = ((bf16[8,13,7168]{2,1,0:T(8,128)(2,1)}), bf16[8,13,7168]{2,1,0:T(8,128)(2,1)}, u32[]{:S(2)}, u32[]{:S(2)}) async-start(bf16[8,13,7168]{2,1,0:T(8,128)(2,1)} %reshape.466), calls=%async_computation | async-start | bytes 3670016 | tf_op jit(solution)/shard_map/all_to_all | solution.py:105
  215.5 14.8 %slice-start = ((s8[7340032]{0:T(1024)(128)(4,1)}), s8[3145728]{0:T(1024)(128)(4,1)S(1)}, s32[]{:S(2)}) async-start(s8[7340032]{0:T(1024)(128)(4,1)} %bitcast.44), calls=%async_computation.9 | async-start | bytes 6291456
  215.5 72.8 %all-to-all-start.2 = ((bf16[4,104,7168]{2,1,0:T(8,128)(2,1)}), bf16[4,104,7168]{2,1,0:T(8,128)(2,1)}, u32[]{:S(2)}, u32[]{:S(2)}) async-start(bf16[4,104,7168]{2,1,0:T(8,128)(2,1)} %bitcast.42), calls=%async_computation.2 | async-start | bytes 11927552 | tf_op jit(solution)/shard_map/all_to_all | solution.py:136
  221.1 9.2 %slice-start.1 = ((s8[7340032]{0:T(1024)(128)(4,1)}), s8[4194304]{0:T(1024)(128)(4,1)S(1)}, s32[]{:S(2)}) async-start(s8[7340032]{0:T(1024)(128)(4,1)} %bitcast.44), calls=%async_computation.10 | async-start | bytes 8388608
  221.1 9.2 %copy-start.3 = (bf16[4,104,7168]{2,1,0:T(8,128)(2,1)S(1)}, bf16[4,104,7168]{2,1,0:T(8,128)(2,1)}, u32[]{:S(2)}) copy-start(bf16[4,104,7168]{2,1,0:T(8,128)(2,1)} %all_to_all.45) | copy-start | bytes 17891332
  288.3 8.8 %copy-start.4 = (f32[416,512]{1,0:T(8,128)S(1)}, f32[416,512]{1,0:T(8,128)}, u32[]{:S(2)}) copy-start(f32[416,512]{1,0:T(8,128)} %fusion.2) | copy-start | bytes 2555908
  288.3 8.8 %copy-start.5 = (f32[416,512]{1,0:T(8,128)S(1)}, f32[416,512]{1,0:T(8,128)}, u32[]{:S(2)}) copy-start(f32[416,512]{1,0:T(8,128)} %fusion.5) | copy-start | bytes 2555908
  308.3 32.6 %all-to-all-start.7 = ((bf16[4,8,13,2]{2,0,3,1:T(4,128)(2,1)}), bf16[4,8,13,2]{2,0,3,1:T(4,128)(2,1)S(1)}, u32[]{:S(2)}, u32[]{:S(2)}) async-start(bf16[4,8,13,2]{2,0,3,1:T(4,128)(2,1)} %copy.135), calls=%async_computation.7 | async-start | bytes 32768 | tf_op jit(solution)/shard_map/all_to_all | solution.py:162
  341.0 136.4 %all-to-all-start.5 = ((bf16[4,8,13,7168]{3,0,2,1:T(4,128)(2,1)}), bf16[4,8,13,7168]{3,0,2,1:T(4,128)(2,1)}, u32[]{:S(2)}, u32[]{:S(2)}) async-start(bf16[4,8,13,7168]{3,0,2,1:T(4,128)(2,1)} %copy.127), calls=%async_computation.5 | async-start | bytes 11927552 | tf_op jit(solution)/shard_map/all_to_all | solution.py:149
  477.4 10.3 %all-to-all-start.8 = ((bf16[4,8,13,2]{2,1,3,0:T(8,128)(2,1)}), bf16[4,8,13,2]{2,1,3,0:T(8,128)(2,1)S(1)}, u32[]{:S(2)}, u32[]{:S(2)}) async-start(bf16[4,8,13,2]{2,1,3,0:T(8,128)(2,1)} %copy.136), calls=%async_computation.8 | async-start | bytes 32768 | tf_op jit(solution)/shard_map/all_to_all | solution.py:161
  487.7 5.7 copy-start.7
  487.7 5.8 copy-start.10
  487.7 6.8 %copy-start.11 = (f32[16,8]{0,1:T(8,128)S(1)}, f32[16,8]{0,1:T(8,128)}, u32[]{:S(2)}) copy-start(f32[16,8]{0,1:T(8,128)} %param.14) | copy-start | bytes 1540
  487.7 72.8 %all-to-all-start.6 = ((bf16[4,8,13,7168]{3,1,2,0:T(8,128)(2,1)}), bf16[4,8,13,7168]{3,1,2,0:T(8,128)(2,1)}, u32[]{:S(2)}, u32[]{:S(2)}) async-start(bf16[4,8,13,7168]{3,1,2,0:T(8,128)(2,1)} %copy.128), calls=%async_computation.6 | async-start | bytes 11927552 | tf_op jit(solution)/shard_map/all_to_all | solution.py:148
  577.0 30.6 %copy-start.1 = (bf16[16,7168]{1,0:T(8,128)(2,1)S(1)}, bf16[16,7168]{1,0:T(8,128)(2,1)}, u32[]{:S(2)}) copy-start(bf16[16,7168]{1,0:T(8,128)(2,1)} %param.12) | copy-start | bytes 688132
where the time goes:
time: 615 us; the launch traced here: 608 us
  waiting for transfers between devices  317 us (52%)
  local copies, waits for them, and re-layouts  105 us (17%)
  blocking collectives  73.8 us (12%)
  matrix products  43.9 us (7%)
  starting transfers between devices  42 us (7%)
  other arithmetic  25.2 us (4%)
    all_to_all x1, waiting for transfers between devices, on_device(): lax.all_to_all(part_dx.reshape(n_local, n_node, cap_exp, width), 'node',...  130 us
    all_to_all x1, blocking collectives, on_device(): lax.all_to_all(out_x.reshape(n_local, n_node * cap_exp, width), 'local',...  73.8 us
    all_to_all x1, waiting for transfers between devices, on_device(): lax.all_to_all(lax.all_to_all(part_dx.reshape(n_local, n_node, cap_exp, w...  63.6 us
    all_to_all x1, waiting for transfers between devices, on_device(): lax.all_to_all(out_dy.reshape(n_local, n_node * cap_exp, width), 'local',...  53.8 us
    all_to_all x1, waiting for transfers between devices, on_device(): lax.all_to_all(send_x, 'node', split_axis=0, concat_axis=0, tiled=True)  40.2 us
    all_to_all x1, waiting for transfers between devices, on_device(): lax.all_to_all(send_dy, 'node', split_axis=0, concat_axis=0, tiled=True)  29.6 us
    gather x2, local copies, waits for them, and re-layouts, finish_slots(): jnp.take(backward_input_gradient.reshape(slots, width), flat_index, axis=0)  19.8 us
    reshape x2, local copies, waits for them, and re-layouts, on_device(): part_dx.reshape(n_local, n_node, cap_exp, width)  17.4 us
  transfers between devices with their start and end apart: 8, of which 5 were waited for; matrix products, arithmetic and copies ran while one was open for 13% of the time, Pallas kernels for 0%

commit v1 on v0

--- a/solution.py
+++ b/solution.py
@@ -185,7 +185,53 @@
     )
 
 
+def on_device_dense(tokens, out_grads, routes, gate_values, gate_weight, up_weight, down_weight):
+    axes = ("node", "local")
+    q = lax.axis_index("node") * lax.axis_size("local") + lax.axis_index("local")
+    picks = jnp.concatenate([routes.astype(jnp.float32), gate_values], axis=1)
+    picks = lax.all_gather(picks, axes, axis=0, tiled=True)
+    rows_x = lax.all_gather(tokens, axes, axis=0, tiled=True)
+    rows_dy = lax.all_gather(out_grads, axes, axis=0, tiled=True)
+    pick_count = routes.shape[1]
+    hot = picks[:, :pick_count] == (q // 2).astype(jnp.float32)
+    weight = jnp.sum(jnp.where(hot, picks[:, pick_count:], 0.0), axis=1)
+    w_gate = gate_weight[0]
+    w_up = up_weight[0]
+    w_down = down_weight[0]
+    pre_gate = jnp.dot(rows_x, w_gate, preferred_element_type=jnp.float32)
+    pre_up = jnp.dot(rows_x, w_up, preferred_element_type=jnp.float32)
+    sigmoid_gate = jax.nn.sigmoid(pre_gate)
+    activated = pre_gate * sigmoid_gate
+    hidden = (activated * pre_up).astype(jnp.bfloat16)
+    back_grad = lax.dot_general(
+        rows_dy, w_down, (((1,), (1,)), ((), ())), preferred_element_type=jnp.float32
+    )
+    part_gate = jnp.sum(hidden.astype(jnp.float32) * back_grad, axis=1)
+    d_gate = back_grad * pre_up * sigmoid_gate * (1.0 + pre_gate * (1.0 - sigmoid_gate))
+    d_up = back_grad * activated
+    part_dx = lax.dot_general(
+        d_gate.astype(jnp.bfloat16),
+        w_gate,
+        (((1,), (1,)), ((), ())),
+        preferred_element_type=jnp.float32,
+    )
+    part_dx = part_dx + lax.dot_general(
+        d_up.astype(jnp.bfloat16),
+        w_up,
+        (((1,), (1,)), ((), ())),
+        preferred_element_type=jnp.float32,
+    )
+    part_dx = jnp.where(weight[:, None] > 0.0, part_dx * weight[:, None], 0.0)
+    gate_terms = jnp.where(hot, part_gate[:, None], 0.0)
+    input_grads = lax.psum_scatter(
+        part_dx.astype(jnp.bfloat16), axes, scatter_dimension=0, tiled=True
+    )
+    gate_grads = lax.psum_scatter(gate_terms, axes, scatter_dimension=0, tiled=True)
+    return input_grads, gate_grads
+
+
 def solution(mesh):
+    devices = mesh.shape["node"] * mesh.shape["local"]
     in_specs = (
         P(("node", "local"), None),
         P(("node", "local"), None),
@@ -196,6 +242,7 @@
         P(("node", "local"), None, None),
     )
     out_specs = (P(("node", "local"), None), P(("node", "local"), None))
+    body = on_device_dense if devices <= 32 else on_device
     return jax.shard_map(
-        on_device, mesh=mesh, in_specs=in_specs, out_specs=out_specs, check_vma=False
-    )
+        body, mesh=mesh, in_specs=in_specs, out_specs=out_specs, check_vma=False
+    )

time: 615 us -> 457 us (0.74); the launches traced: 608 us -> 457 us
  local copies, waits for them, and re-layouts: 105 us -> 1.43 us
  starting transfers between devices: 42 us -> 0.34 us
  blocking collectives: 73.8 us -> 44.4 us
  waiting for transfers between devices: 317 us -> 345 us
  other arithmetic: 25.2 us -> 2.45 us
  between operations: 1.27 us -> 13.8 us
    all_to_all x8 -> x0, waiting for transfers between devices: 317 us -> none  [the longest x1 130 us: on_device(): lax.all_to_all(part_dx.reshape(n_local, n_node, cap_exp, width), 'node',...]
    reduce_scatter x0 -> x1, waiting for transfers between devices: none -> 144 us  [on_device_dense(): lax.psum_scatter(part_dx.astype(jnp.bfloat16), axes, scatter_dimension=0,...]
    unnamed x0 -> x5, waiting for transfers between devices: none -> 109 us
    all_gather x0 -> x2, waiting for transfers between devices: none -> 91.8 us  [the longest x1 59.1 us: on_device_dense(): rows_dy = lax.all_gather(out_grads, axes, axis=0, tiled=True)]
    all_to_all x1 -> x0, blocking collectives: 73.8 us -> none  [on_device(): lax.all_to_all(out_x.reshape(n_local, n_node * cap_exp, width), 'local',...]
    all_gather x0 -> x1, blocking collectives: none -> 44.4 us  [on_device_dense(): picks = lax.all_gather(picks, axes, axis=0, tiled=True)]
    all_to_all x8 -> x0, starting transfers between devices: 42 us -> none  [the longest x1 7.25 us: on_device(): lax.all_to_all(slot_codes, 'node', split_axis=0, concat_axis=0, tiled=True)]
    gather x7 -> x0, local copies, waits for them, and re-layouts: 39 us -> none  [the longest x2 19.8 us: finish_slots(): jnp.take(backward_input_gradient.reshape(slots, width), flat_index, axis=0)]
  transfers between devices with their start and end apart: 8 -> 4, of which waited for: 5 -> 4; matrix products, arithmetic and copies ran while one was open for 13% -> 9% of each run, Pallas kernels for 0% -> 0%
where the time goes in v1:
time: 457 us
  waiting for transfers between devices  345 us (75%)
  matrix products  48.8 us (11%)
  blocking collectives  44.4 us (10%)
  between operations  13.8 us (3%)
    reduce_scatter x1, waiting for transfers between devices, on_device_dense(): lax.psum_scatter(part_dx.astype(jnp.bfloat16), axes, scatter_dimension=0,...  144 us
    unnamed x5, waiting for transfers between devices  109 us
    all_gather x1, waiting for transfers between devices, on_device_dense(): rows_dy = lax.all_gather(out_grads, axes, axis=0, tiled=True)  59.1 us
    all_gather x1, blocking collectives, on_device_dense(): picks = lax.all_gather(picks, axes, axis=0, tiled=True)  44.4 us
    all_gather x1, waiting for transfers between devices, on_device_dense(): rows_x = lax.all_gather(tokens, axes, axis=0, tiled=True)  32.7 us
    dot_general x1, matrix products, on_device_dense(): lax.dot_general(d_up.astype(jnp.bfloat16), w_up, (((1,), (1,)), ((), ()))...  13.8 us
    dot_general x1, matrix products, on_device_dense(): lax.dot_general(d_gate.astype(jnp.bfloat16), w_gate, (((1,), (1,)), ((),...  10.7 us
    dot_general x1, matrix products, on_device_dense(): pre_gate = jnp.dot(rows_x, w_gate, preferred_element_type=jnp.float32)  9.29 us
  transfers between devices with their start and end apart: 4, of which 4 were waited for; matrix products, arithmetic and copies ran while one was open for 9% of the time, Pallas kernels for 0%

profile of v1, /device:TPU:0, one launch (start us, length us, event | category | flops | bytes accessed | tf_op | source)
XLA Modules:
  0.0 456.5 jit_solution(3514259724453034477)
XLA Ops:
  7.2 0.0 all-gather.5.cloned.1.call-start
  7.2 0.7 all-gather.5.cloned.1.call-update
  7.9 0.0 all-gather.3.cloned.1.call-start
  7.9 0.7 all-gather.3.cloned.1.call-update
  8.6 0.0 reduce-scatter.7.cloned.1.call-start
  8.7 0.7 convert_element_type.21
  9.4 0.7 pad_maximum_fusion
  10.1 0.1 copy.12
  10.2 44.4 %all_gather.9 = f32[512,16]{1,0:T(8,128)S(1)} all-gather(f32[16,16]{1,0:T(8,128)S(1)} %copy.12), channel_id=1, replica_groups=mesh['node'=8,'local'=4] {'node','local'}, dimensions={0}, use_global_device_ids=true | all-gather | bytes 33792 | tf_op jit(solution)/shard_map/all_gather | solution.py:192
  54.6 32.7 %all-gather.5.cloned.1.call-done = bf16[512,7168]{1,0:T(8,128)(2,1)} async-done(((bf16[16,7168]{1,0:T(8,128)(2,1)}), bf16[512,7168]{1,0:T(8,128)(2,1)}) %all-gather.5.cloned.1.call-update) | async-done | bytes 7340048 | tf_op jit(solution)/shard_map/all_gather | solution.py:193
  87.3 9.3 %fusion.2 = f32[512,512]{0,1:T(8,128)S(1)} fusion(bf16[512,7168]{1,0:T(8,128)(2,1)} %all-gather.5.cloned.1.call-done, bf16[1,7168,512]{2,1,0:T(8,128)(2,1)} %param.11), kind=kOutput, calls=%fused_computation.3 | convolution fusion | flops 3758096384 | bytes 15728640 | tf_op jit(solution)/shard_map/dot_general | solution.py:201
  96.6 6.5 %fusion.5 = f32[512,512]{0,1:T(8,128)S(1)} fusion(bf16[512,7168]{1,0:T(8,128)(2,1)S(1)} %copy-done, bf16[1,7168,512]{2,1,0:T(8,128)(2,1)} %param.12), kind=kOutput, calls=%fused_computation.6 | convolution fusion | flops 3758096384 | bytes 15728640 | tf_op jit(solution)/shard_map/dot_general | solution.py:202
  103.1 59.1 %all-gather.3.cloned.1.call-done = bf16[512,7168]{1,0:T(8,128)(2,1)} async-done(((bf16[16,7168]{1,0:T(8,128)(2,1)}), bf16[512,7168]{1,0:T(8,128)(2,1)}) %all-gather.3.cloned.1.call-update) | async-done | bytes 7340048 | tf_op jit(solution)/shard_map/all_gather | solution.py:194
  162.2 8.5 %multiply_reduce_fusion = (f32[512]{0:T(512)S(1)}, f32[512,512]{0,1:T(8,128)S(1)}) fusion(f32[512,512]{0,1:T(8,128)S(1)} %fusion.5, f32[512,512]{0,1:T(8,128)S(1)} %fusion.2, bf16[512,7168]{1,0:T(8,128)(2,1)} %all-gather.3.cloned.1.call-done, bf16[1,512,7168]{2,1,0:T(8,128)(2,1)} %param.13), kind=kOutput, calls=%fused_computation.10 | convolution fusion | flops 3760455168 | bytes 17827840 | tf_op jit(solution)/shard_map/dot_general | solution.py:206
  170.7 0.8 broadcast_select_fusion
  171.5 0.2 fusion.11
  171.8 0.0 reduce-scatter.7.cloned.1.call-update
  171.8 0.2 reduce-scatter.5.cloned.1.call-start
  172.0 10.7 %fusion = f32[512,7168]{1,0:T(8,128)} fusion(bf16[1,7168,512]{2,1,0:T(8,128)(2,1)} %param.11, f32[512,512]{0,1:T(8,128)S(1)} %fusion.2, f32[512,512]{0,1:T(8,128)S(1)} %get-tuple-element.5, f32[512,512]{0,1:T(8,128)S(1)} %fusion.5), kind=kOutput, calls=%fused_computation.1 | convolution fusion | flops 3760717824 | bytes 25165824 | tf_op jit(solution)/shard_map/dot_general | solution.py:212
  182.7 13.8 %select_convert_fusion = bf16[512,7168]{1,0:T(8,128)(2,1)} fusion(f32[512,7168]{1,0:T(8,128)} %fusion, bf16[1,7168,512]{2,1,0:T(8,128)(2,1)} %param.12, f32[512]{0:T(512)S(1)} %fusion.11, pred[512]{0:T(512)(128)(4,1)S(1)} %broadcast_compare_fusion, f32[512,512]{0,1:T(8,128)S(1)} %get-tuple-element.5, f32[512,512]{0,1:T(8,128)S(1)} %fusion.2), kind=kOutput, calls=%fused_computation | convolution fusion | flops 3774349312 | bytes 31459840 | tf_op jit(solution)/shard_map/dot_general | solution.py:218
  196.6 0.0 reduce-scatter.5.cloned.1.call-update
  196.6 107.7 %reduce-scatter.7.cloned.1.call-done = f32[16,8]{1,0:T(8,128)} async-done(((f32[512,8]{1,0:T(8,128)}), f32[16,8]{1,0:T(8,128)}) %reduce-scatter.7.cloned.1.call-update) | async-done | bytes 528
  304.3 1.4 copy.15
  305.7 144.3 %reduce-scatter.5.cloned.1.call-done = bf16[16,7168]{1,0:T(8,128)(2,1)} async-done(((bf16[512,7168]{1,0:T(8,128)(2,1)}), bf16[16,7168]{1,0:T(8,128)(2,1)}) %reduce-scatter.5.cloned.1.call-update) | async-done | bytes 229392 | tf_op jit(solution)/shard_map/reduce_scatter | solution.py:226
  (3 shorter events, 0.0 us)
Async XLA Ops:
  7.2 80.1 %all-gather.5.cloned.1.call-start = ((), (), s32[]{:S(2)}) async-start(), calls=%async_computation.3 | async-start | bytes 7569408 | tf_op jit(solution)/shard_map/all_gather | solution.py:193
  7.9 154.3 %all-gather.3.cloned.1.call-start = ((), (), s32[]{:S(2)}) async-start(), calls=%async_computation.2 | async-start | bytes 7569408 | tf_op jit(solution)/shard_map/all_gather | solution.py:194
  8.6 295.7 %reduce-scatter.7.cloned.1.call-start = ((), (), s32[]{:S(2)}) async-start(), calls=%async_computation.5 | async-start | bytes 270336
  87.3 9.3 %copy-start = (bf16[512,7168]{1,0:T(8,128)(2,1)S(1)}, bf16[512,7168]{1,0:T(8,128)(2,1)}, u32[]{:S(2)}) copy-start(bf16[512,7168]{1,0:T(8,128)(2,1)} %all-gather.5.cloned.1.call-done) | copy-start | bytes 22020100
  171.8 278.2 %reduce-scatter.5.cloned.1.call-start = ((), (), s32[]{:S(2)}) async-start(), calls=%async_computation.4 | async-start | bytes 7569408 | tf_op jit(solution)/shard_map/reduce_scatter | solution.py:226
Sparse Core Ops, SparseCore 0:
  10.9 76.3 all-gather.4
  90.2 71.9 all-gather.2
  171.9 132.3 reduce-scatter.6
  307.2 142.7 reduce-scatter.4

commit v2 on v0

--- a/solution.py
+++ b/solution.py
@@ -1,10 +1,14 @@
 import jax
 import jax.numpy as jnp
 from jax import lax
+from jax.experimental import pallas as pl
+from jax.experimental.pallas import tpu as pltpu
 from jax.sharding import PartitionSpec as P
 
 NODE_LIMIT = 4
 PER_NODE = 2
+MESH = pl.DeviceIdType.MESH
+NT = (((1,), (1,)), ((), ()))
 
 
 def shard_terms(rows_x, rows_dy, w_gate, w_up, w_down):
@@ -185,7 +189,379 @@
     )
 
 
+def pair_kernel(
+    tok, dyo, aux, wg_hbm, wu_hbm, wd_hbm, dx_out, gate_out,
+    gx, gdy, wg, wu, wd, pg, pu, bg, dg, du, part, from_sib, from_one, from_two, from_z,
+    local_sem, ag_send, ag_recv, rs_send, rs_recv,
+):
+    width = tok.shape[1]
+    node = lax.axis_index("node")
+    local = lax.axis_index("local")
+    z, x = node // 2, node % 2
+    y, core = local // 2, local % 2
+    sib = (node, y * 2 + (1 - core))
+    x_nbr = (z * 2 + (1 - x), local)
+    y_nbr = (node, (1 - y) * 2 + core)
+    z_peer = [None] + [(((z + k) % 4) * 2 + x, local) for k in (1, 2, 3)]
+    expert = (node * 4 + local) // 2
+
+    weight_copies = [
+        pltpu.make_async_copy(src, dst, local_sem.at[i])
+        for i, (src, dst) in enumerate(((wg_hbm, wg), (wu_hbm, wu), (wd_hbm, wd)))
+    ]
+    own_copies = [
+        pltpu.make_async_copy(tok, gx.at[pl.ds(0, 16), pl.ds(0, width)], local_sem.at[3]),
+        pltpu.make_async_copy(aux, gx.at[pl.ds(0, 16), pl.ds(width, 128)], local_sem.at[4]),
+        pltpu.make_async_copy(dyo, gdy.at[pl.ds(0, 16), :], local_sem.at[5]),
+    ]
+    for c in own_copies:
+        c.start()
+
+    barrier = pltpu.get_barrier_semaphore()
+    for dev in [sib, x_nbr, y_nbr] + z_peer[1:]:
+        pl.semaphore_signal(barrier, inc=1, device_id=dev, device_id_type=MESH)
+    pl.semaphore_wait(barrier, 6)
+    for c in own_copies:
+        c.wait()
+
+    buffers = (gx, gdy)
+    first_nbr = (x_nbr, y_nbr)
+    second_nbr = (y_nbr, x_nbr)
+    sends = []
+    counts = [0, 0]
+
+    def slot(second, dc, first, r):
+        return second * 16 + dc * 8 + first * 4 + r
+
+    def block(a, s):
+        return buffers[a].at[pl.ds(s * 16, 16), :]
+
+    def push(a, src, dst, dev):
+        c = pltpu.make_async_remote_copy(
+            src_ref=block(a, src),
+            dst_ref=block(a, dst),
+            send_sem=ag_send.at[a, counts[a]],
+            recv_sem=ag_recv.at[a, dst],
+            device_id=dev,
+            device_id_type=MESH,
+        )
+        counts[a] += 1
+        c.start()
+        sends.append(c)
+
+    def arrived(a, s):
+        pltpu.make_async_remote_copy(
+            src_ref=block(a, s),
+            dst_ref=block(a, s),
+            send_sem=ag_send.at[a, 0],
+            recv_sem=ag_recv.at[a, s],
+            device_id=sib,
+            device_id_type=MESH,
+        ).wait_recv()
+
+    def spread(a, second, first, r):
+        src = slot(second, 0, first, r)
+        if second == 0 and first == 0:
+            push(a, src, slot(0, 0, 1, r), first_nbr[a])
+        if second == 0:
+            push(a, src, slot(1, 0, first, r), second_nbr[a])
+        push(a, src, slot(second, 1, first, r), sib)
+
+    for k in (1, 2, 3):
+        for a in (0, 1):
+            push(a, 0, slot(0, 0, 0, 4 - k), z_peer[k])
+    for a in (0, 1):
+        spread(a, 0, 0, 0)
+    for c in weight_copies:
+        c.start()
+    order = (0, 1, 3, 2)
+    for r in order[1:]:
+        for a in (0, 1):
+            arrived(a, slot(0, 0, 0, r))
+            spread(a, 0, 0, r)
+    for r in order:
+        for a in (0, 1):
+            arrived(a, slot(0, 0, 1, r))
+            spread(a, 0, 1, r)
+
+    step = 1792
+
+    def forward(half):
+        rows = pl.ds(half * 256, 256)
+        for acc, w in ((pg, wg), (pu, wu)):
+            acc[rows, :] = jnp.zeros((256, 512), jnp.float32)
+
+        def body(k, carry):
+            cols = pl.ds(pl.multiple_of(k * step, 256), step)
+            left = gx[rows, cols]
+            pg[rows, :] += jnp.dot(left, wg[cols, :], preferred_element_type=jnp.float32)
+            pu[rows, :] += jnp.dot(left, wu[cols, :], preferred_element_type=jnp.float32)
+            return carry
+
+        lax.fori_loop(0, width // step, body, 0)
+
+    def backward(half):
+        rows = pl.ds(half * 256, 256)
+        bg[rows, :] = jnp.zeros((256, 512), jnp.float32)
+
+        def body(k, carry):
+            cols = pl.ds(pl.multiple_of(k * step, 256), step)
+            bg[rows, :] += lax.dot_general(
+                gdy[rows, cols], wd[:, cols], NT, preferred_element_type=jnp.float32
+            )
+            return carry
+
+        lax.fori_loop(0, width // step, body, 0)
+
+    for c in weight_copies:
+        c.wait()
+    for a in (0, 1):
+        for first in (0, 1):
+            for r in order:
+                arrived(a, slot(0, 1, first, r))
+        (forward, backward)[a](0)
+    for first in (0, 1):
+        for r in order:
+            for a in (0, 1):
+                arrived(a, slot(1, 0, first, r))
+                spread(a, 1, first, r)
+    for a in (0, 1):
+        for first in (0, 1):
+            for r in order:
+                arrived(a, slot(1, 1, first, r))
+        (forward, backward)[a](1)
+
+    lane = lax.broadcasted_iota(jnp.int32, (64, 128), 1)
+    for dc in (1, 0):
+        for dy in (0, 1):
+            for dx in (0, 1):
+                at_x = pl.ds((dy * 4 + dc * 2 + dx) * 64, 64)
+                at_dy = pl.ds((dx * 4 + dc * 2 + dy) * 64, 64)
+                group = dc * 4 + dy * 2 + dx
+                at = pl.ds(group * 64, 64)
+                info = gx[at_x, pl.ds(width, 128)].astype(jnp.float32)
+                hot = (lane % 16 == expert) & (lane < 48)
+                weight = jnp.sum(jnp.where(hot, info, 0.0), axis=1, keepdims=True)
+                pick = jnp.sum(
+                    jnp.where(lane == 48 + expert, info, 0.0), axis=1, keepdims=True
+                )
+                pre_gate = pg[at_x, :]
+                pre_up = pu[at_x, :]
+                back = bg[at_dy, :]
+                sig = jax.nn.sigmoid(pre_gate)
+                act = pre_gate * sig
+                hidden = (act * pre_up).astype(jnp.bfloat16).astype(jnp.float32)
+                part_gate = jnp.sum(hidden * back, axis=1, keepdims=True)
+                dg[at, :] = (
+                    weight * (back * pre_up * sig * (1.0 + pre_gate * (1.0 - sig)))
+                ).astype(jnp.bfloat16)
+                du[at, :] = (weight * (back * act)).astype(jnp.bfloat16)
+                term = jnp.where(
+                    (lane + 1).astype(jnp.float32) == pick, jnp.broadcast_to(part_gate, (64, 128)), 0.0
+                )
+                high = term.astype(jnp.bfloat16)
+                low = (term - high.astype(jnp.float32)).astype(jnp.bfloat16)
+                blocks = pl.ds(group * 4, 4)
+                part[blocks, :, pl.ds(width, 128)] = high.reshape(4, 16, 128)
+                part[blocks, :, pl.ds(width + 128, 128)] = low.reshape(4, 16, 128)
+
+    quarter = width // 4
+    pieces = [pl.ds(p * quarter, quarter + (256 if p == 3 else 0)) for p in range(4)]
+
+    def product(dc, p):
+        rows = pl.ds(dc * 256, 256)
+
+        def body(n, carry):
+            cols = pl.ds(pl.multiple_of(p * quarter + n * 256, 256), 256)
+            out = lax.dot_general(
+                dg[rows, :], wg[cols, :], NT, preferred_element_type=jnp.float32
+            ) + lax.dot_general(du[rows, :], wu[cols, :], NT, preferred_element_type=jnp.float32)
+            part[pl.ds(dc * 16, 16), :, cols] = out.astype(jnp.bfloat16).reshape(16, 16, 256)
+            return carry
+
+        lax.fori_loop(0, quarter // 256, body, 0)
+
+    def rs_copy(p, lane_at, src, dst, dev):
+        return pltpu.make_async_remote_copy(
+            src_ref=src,
+            dst_ref=dst,
+            send_sem=rs_send.at[p, lane_at],
+            recv_sem=rs_recv.at[p, lane_at],
+            device_id=dev,
+            device_id_type=MESH,
+        )
+
+    def add(base, got, got_base, n, cols):
+        def body(i, carry):
+            total = part[base + i, :, cols].astype(jnp.float32) + got[
+                got_base + i, :, cols
+            ].astype(jnp.float32)
+            part[base + i, :, cols] = total.astype(jnp.bfloat16)
+            return carry
+
+        lax.fori_loop(0, n, body, 0)
+
+    flight = {}
+
+    def launch(p, name, *copies):
+        for c in copies:
+            c.start()
+            sends.append(c)
+        flight[p, name] = copies
+
+    def landed(p, name):
+        for c in flight[p, name]:
+            c.wait_recv()
+
+    def stage_sib(p):
+        cols = pieces[p]
+        launch(p, 0, rs_copy(p, 0, part.at[pl.ds(16, 16), :, cols], from_sib.at[:, :, cols], sib))
+
+    def stage_one(p):
+        cols = pieces[p]
+        landed(p, 0)
+        add(0, from_sib, 0, 16, pl.ds(p * quarter, quarter))
+        if p == 3:
+            hi, lo = pl.ds(width, 128), pl.ds(width + 128, 128)
+
+            def body(i, carry):
+                total = (
+                    part[i, :, hi].astype(jnp.float32)
+                    + part[i, :, lo].astype(jnp.float32)
+                    + from_sib[i, :, hi].astype(jnp.float32)
+                    + from_sib[i, :, lo].astype(jnp.float32)
+                )
+                high = total.astype(jnp.bfloat16)
+                part[i, :, hi] = high
+                part[i, :, lo] = (total - high.astype(jnp.float32)).astype(jnp.bfloat16)
+                return carry
+
+            lax.fori_loop(0, 16, body, 0)
+        if p % 2 == 0:
+            launch(p, 1, rs_copy(p, 1, part.at[pl.ds(8, 8), :, cols], from_one.at[:, :, cols], y_nbr))
+        else:
+            launch(
+                p,
+                1,
+                rs_copy(p, 1, part.at[pl.ds(4, 4), :, cols], from_one.at[pl.ds(0, 4), :, cols], x_nbr),
+                rs_copy(p, 2, part.at[pl.ds(12, 4), :, cols], from_one.at[pl.ds(4, 4), :, cols], x_nbr),
+            )
+
+    def stage_two(p):
+        cols = pieces[p]
+        landed(p, 1)
+        if p % 2 == 0:
+            add(0, from_one, 0, 8, cols)
+            launch(p, 2, rs_copy(p, 3, part.at[pl.ds(4, 4), :, cols], from_two.at[:, :, cols], x_nbr))
+        else:
+            add(0, from_one, 0, 4, cols)
+            add(8, from_one, 4, 4, cols)
+            launch(p, 2, rs_copy(p, 3, part.at[pl.ds(8, 4), :, cols], from_two.at[:, :, cols], y_nbr))
+
+    def stage_three(p):
+        cols = pieces[p]
+        landed(p, 2)
+        add(0, from_two, 0, 4, cols)
+        launch(
+            p,
+            3,
+            *[
+                rs_copy(p, 3 + r, part.at[r, :, cols], from_z.at[r - 1, :, cols], z_peer[r])
+                for r in (2, 1, 3)
+            ],
+        )
+
+    def stage_last(p):
+        landed(p, 3)
+
+        def total(cols):
+            return (
+                part[0, :, cols].astype(jnp.float32)
+                + from_z[0, :, cols].astype(jnp.float32)
+                + from_z[1, :, cols].astype(jnp.float32)
+                + from_z[2, :, cols].astype(jnp.float32)
+            )
+
+        cols = pl.ds(p * quarter, quarter)
+        dx_out[:, cols] = total(cols).astype(jnp.bfloat16)
+        if p == 3:
+            gate_out[...] = total(pl.ds(width, 128)) + total(pl.ds(width + 128, 128))
+
+    for p in range(4):
+        product(1, p)
+        stage_sib(p)
+        product(0, p)
+        stage_one(p)
+    for pair in ((0, 1), (2, 3)):
+        for stage in (stage_two, stage_three):
+            for p in pair:
+                stage(p)
+    for p in range(4):
+        stage_last(p)
+    for c in sends:
+        c.wait_send()
+
+
+def on_device_kernel(tokens, out_grads, routes, gate_values, gate_weight, up_weight, down_weight):
+    rows, width = tokens.shape
+    experts = lax.axis_size("node") * lax.axis_size("local") // 2
+    hot = routes[:, :, None] == jnp.arange(experts, dtype=jnp.int32)[None, None, :]
+    table = jnp.sum(jnp.where(hot, gate_values[:, :, None], 0.0), axis=1)
+    high = lax.reduce_precision(table, 8, 7)
+    mid = lax.reduce_precision(table - high, 8, 7)
+    low = table - high - mid
+    picks = jnp.arange(1, routes.shape[1] + 1, dtype=jnp.float32)[None, :, None]
+    pick = jnp.sum(jnp.where(hot, picks, 0.0), axis=1)
+    aux = jnp.concatenate([high, mid, low, pick], axis=1)
+    aux = jnp.pad(aux, ((0, 0), (0, 128 - 4 * experts))).astype(jnp.bfloat16)
+    half = gate_weight.shape[2]
+    total = width + 256
+    bf16, f32 = jnp.bfloat16, jnp.float32
+    dx, gate = pl.pallas_call(
+        pair_kernel,
+        out_shape=(
+            jax.ShapeDtypeStruct((rows, width), bf16),
+            jax.ShapeDtypeStruct((rows, 128), f32),
+        ),
+        in_specs=[pl.BlockSpec(memory_space=pl.ANY)] * 6,
+        out_specs=(
+            pl.BlockSpec(memory_space=pltpu.VMEM),
+            pl.BlockSpec(memory_space=pltpu.VMEM),
+        ),
+        scratch_shapes=[
+            pltpu.VMEM((512, width + 128), bf16),
+            pltpu.VMEM((512, width), bf16),
+            pltpu.VMEM((width, half), bf16),
+            pltpu.VMEM((width, half), bf16),
+            pltpu.VMEM((half, width), bf16),
+            pltpu.VMEM((512, half), f32),
+            pltpu.VMEM((512, half), f32),
+            pltpu.VMEM((512, half), f32),
+            pltpu.VMEM((512, half), bf16),
+            pltpu.VMEM((512, half), bf16),
+            pltpu.VMEM((32, 16, total), bf16),
+            pltpu.VMEM((16, 16, total), bf16),
+            pltpu.VMEM((8, 16, total), bf16),
+            pltpu.VMEM((4, 16, total), bf16),
+            pltpu.VMEM((3, 16, total), bf16),
+            pltpu.SemaphoreType.DMA((6,)),
+            pltpu.SemaphoreType.DMA((2, 32)),
+            pltpu.SemaphoreType.DMA((2, 32)),
+            pltpu.SemaphoreType.DMA((4, 8)),
+            pltpu.SemaphoreType.DMA((4, 8)),
+        ],
+        compiler_params=pltpu.CompilerParams(
+            collective_id=0, has_side_effects=True, vmem_limit_bytes=62 * 1024 * 1024
+        ),
+        cost_estimate=pl.CostEstimate(
+            flops=10 * 512 * width * half, bytes_accessed=6 * width * half, transcendentals=0
+        ),
+    )(tokens, out_grads, aux, gate_weight[0], up_weight[0], down_weight[0])
+    return dx, gate[:, : routes.shape[1]]
+
+
 def solution(mesh):
+    small = mesh.shape["node"] == 8 and mesh.shape["local"] == 4
     in_specs = (
         P(("node", "local"), None),
         P(("node", "local"), None),
@@ -196,6 +572,7 @@
         P(("node", "local"), None, None),
     )
     out_specs = (P(("node", "local"), None), P(("node", "local"), None))
+    body = on_device_kernel if small else on_device
     return jax.shard_map(
-        on_device, mesh=mesh, in_specs=in_specs, out_specs=out_specs, check_vma=False
-    )
+        body, mesh=mesh, in_specs=in_specs, out_specs=out_specs, check_vma=False
+    )

time: 615 us -> 162 us (0.26); the launches traced: 608 us -> 161 us
  waiting for transfers between devices: 317 us -> 0 us
  Pallas kernels: 0 us -> 155 us
  local copies, waits for them, and re-layouts: 105 us -> 4.51 us
  blocking collectives: 73.8 us -> 0 us
  matrix products: 43.9 us -> 0 us
  starting transfers between devices: 42 us -> 0 us
  other arithmetic: 25.2 us -> 0.82 us
    all_to_all x8 -> x0, waiting for transfers between devices: 317 us -> none  [the longest x1 130 us: on_device(): lax.all_to_all(part_dx.reshape(n_local, n_node, cap_exp, width), 'node',...]
    pallas_call x0 -> x1, Pallas kernels: none -> 155 us  [on_device_kernel(): pl.pallas_call(pair_kernel, out_shape=(jax.ShapeDtypeStruct((rows, width)...]
    all_to_all x1 -> x0, blocking collectives: 73.8 us -> none  [on_device(): lax.all_to_all(out_x.reshape(n_local, n_node * cap_exp, width), 'local',...]
    dot_general x5 -> x0, matrix products: 43.9 us -> none  [the longest x1 11.3 us: shard_terms(): lax.dot_general(d_up, w_up, (((1,), (1,)), ((), ())), preferred_element_t...]
    all_to_all x8 -> x0, starting transfers between devices: 42 us -> none  [the longest x1 7.25 us: on_device(): lax.all_to_all(slot_codes, 'node', split_axis=0, concat_axis=0, tiled=True)]
    gather x7 -> x0, local copies, waits for them, and re-layouts: 39 us -> none  [the longest x2 19.8 us: finish_slots(): jnp.take(backward_input_gradient.reshape(slots, width), flat_index, axis=0)]
    reshape x15 -> x0, local copies, waits for them, and re-layouts: 32.7 us -> none  [the longest x2 17.4 us: on_device(): part_dx.reshape(n_local, n_node, cap_exp, width)]
    all_to_all x4 -> x0, local copies, waits for them, and re-layouts: 16.6 us -> none  [the longest x1 8.98 us: on_device(): lax.all_to_all(lax.all_to_all(part_dx.reshape(n_local, n_node, cap_exp, w...]
  transfers between devices with their start and end apart: 8 -> 0, of which waited for: 5 -> 0; matrix products, arithmetic and copies ran while one was open for 13% -> 0% of each run, Pallas kernels for 0% -> 0%
where the time goes in v2:
time: 162 us; the launch traced here: 161 us
  Pallas kernels  155 us (96%)
  local copies, waits for them, and re-layouts  4.51 us (3%)
    pallas_call x1, Pallas kernels, on_device_kernel(): pl.pallas_call(pair_kernel, out_shape=(jax.ShapeDtypeStruct((rows, width)...  155 us
    unnamed x4, local copies, waits for them, and re-layouts  4.51 us

profile of v2, /device:TPU:0, one launch (start us, length us, event | category | flops | bytes accessed | tf_op | source)
XLA Modules:
  0.0 161.4 jit_solution(3669548718419652277)
XLA Ops:
  0.6 0.8 copy.12
  1.4 0.8 copy.13
  2.2 0.1 select_reduce_fusion.1
  2.3 0.7 fusion.7.aux
  3.0 155.4 %shard_map.86 = (bf16[16,7168]{1,0:T(8,128)(2,1)}, f32[16,128]{1,0:T(8,128)}) custom-call(bf16[16,7168]{1,0:T(8,128)(2,1)} %tok.1, bf16[16,7168]{1,0:T(8,128)(2,1)} %dyo.1, bf16[16,128]{1,0:T(8,128)(2,1)} %fusion.7.aux, bf16[7168,512]{1,0:T(8,128)(2,1)} %bitcast.5, bf16[7168,512]{1,0:T(8,128)(2,1)} %bitcast.6, bf16[512,7168]{1,0:T(8,128)(2,1)} %bitcast.7), custom_call_target="tpu_custom_call" | custom-call | flops 18790481920 | bytes 22020096 | tf_op jit(solution)/shard_map/pallas_call | solution.py:520
  158.4 1.4 copy.14
  159.8 1.6 %copy.16 = bf16[16,7168]{1,0:T(8,128)(2,1)} copy(bf16[16,7168]{1,0:T(8,128)(2,1)} %get-tuple-element.17) | data formatting | bytes 458752
  (2 shorter events, 0.0 us)

commit v3 on v2

--- a/solution.py
+++ b/solution.py
@@ -227,109 +227,197 @@
     buffers = (gx, gdy)
     first_nbr = (x_nbr, y_nbr)
     second_nbr = (y_nbr, x_nbr)
+    early = 1024
     sends = []
-    counts = [0, 0]
+    counts = [0, 0, 0, 0]
 
     def slot(second, dc, first, r):
         return second * 16 + dc * 8 + first * 4 + r
 
-    def block(a, s):
-        return buffers[a].at[pl.ds(s * 16, 16), :]
-
-    def push(a, src, dst, dev):
+    def block(a, e, s):
+        whole = buffers[a].shape[1]
+        cols = pl.ds(0, early) if e == 0 else pl.ds(early, whole - early)
+        return buffers[a].at[pl.ds(pl.multiple_of(s * 16, 16), 16), cols]
+
+    def push(a, e, src, dst, dev, cond=None):
+        kind = a * 2 + e
         c = pltpu.make_async_remote_copy(
-            src_ref=block(a, src),
-            dst_ref=block(a, dst),
-            send_sem=ag_send.at[a, counts[a]],
-            recv_sem=ag_recv.at[a, dst],
+            src_ref=block(a, e, src),
+            dst_ref=block(a, e, dst),
+            send_sem=ag_send.at[kind, counts[kind]],
+            recv_sem=ag_recv.at[kind, dst],
             device_id=dev,
             device_id_type=MESH,
         )
-        counts[a] += 1
-        c.start()
-        sends.append(c)
-
-    def arrived(a, s):
+        counts[kind] += 1
+        if cond is None:
+            c.start()
+        else:
+            pl.when(cond)(c.start)
+        sends.append((cond, c))
+
+    def arrived(a, e, s):
         pltpu.make_async_remote_copy(
-            src_ref=block(a, s),
-            dst_ref=block(a, s),
-            send_sem=ag_send.at[a, 0],
-            recv_sem=ag_recv.at[a, s],
+            src_ref=block(a, e, s),
+            dst_ref=block(a, e, s),
+            send_sem=ag_send.at[a * 2 + e, 0],
+            recv_sem=ag_recv.at[a * 2 + e, s],
             device_id=sib,
             device_id_type=MESH,
         ).wait_recv()
 
-    def spread(a, second, first, r):
-        src = slot(second, 0, first, r)
-        if second == 0 and first == 0:
-            push(a, src, slot(0, 0, 1, r), first_nbr[a])
-        if second == 0:
-            push(a, src, slot(1, 0, first, r), second_nbr[a])
-        push(a, src, slot(second, 1, first, r), sib)
-
-    for k in (1, 2, 3):
-        for a in (0, 1):
-            push(a, 0, slot(0, 0, 0, 4 - k), z_peer[k])
-    for a in (0, 1):
-        spread(a, 0, 0, 0)
+    def chain_own(a, e, second, first):
+        base = slot(second, 0, first, 0)
+        push(a, e, base, base + 3, (node + 2, local), z < 3)
+        push(a, e, base, base + 1, (node - 2, local), z > 0)
+
+    def chain(a, e, second, first, r):
+        base = slot(second, 0, first, 0)
+        up = z + r >= 4
+        target = jnp.where(up, node + 2, node - 2)
+        onward = (up & (z < 3)) | (jnp.logical_not(up) & (z > 0))
+        push(a, e, base + r, base + jnp.where(up, r - 1, r + 1), (target, local), onward)
+
+    def to_first(a, e, second, first, r):
+        push(a, e, slot(second, 0, first, r), slot(second, 0, 1, r), first_nbr[a])
+
+    def to_second(a, e, second, first, r):
+        push(a, e, slot(second, 0, first, r), slot(1, 0, first, r), second_nbr[a])
+
+    def to_sib(a, e, second, first, r):
+        push(a, e, slot(second, 0, first, r), slot(second, 1, first, r), sib)
+
+    middle = (z == 1) | (z == 2)
+    far = (
+        jnp.where(z == 3, 3, 1),
+        jnp.where(middle, 3, 2),
+        jnp.where(middle, 2, jnp.where(z == 0, 3, 1)),
+    )
+    both = (0, 1)
+
+    for a in both:
+        chain_own(a, 1, 0, 0)
+    for a in both:
+        to_first(a, 0, 0, 0, 0)
+    for a in both:
+        to_second(a, 0, 0, 0, 0)
+    for a in both:
+        to_first(a, 1, 0, 0, 0)
+    for a in both:
+        to_second(a, 1, 0, 0, 0)
+    for a in both:
+        chain_own(a, 0, 0, 0)
+    for a in both:
+        to_sib(a, 1, 0, 0, 0)
+        to_sib(a, 0, 0, 0, 0)
     for c in weight_copies:
         c.start()
-    order = (0, 1, 3, 2)
-    for r in order[1:]:
-        for a in (0, 1):
-            arrived(a, slot(0, 0, 0, r))
-            spread(a, 0, 0, r)
-    for r in order:
-        for a in (0, 1):
-            arrived(a, slot(0, 0, 1, r))
-            spread(a, 0, 1, r)
-
-    step = 1792
-
-    def forward(half):
-        rows = pl.ds(half * 256, 256)
-        for acc, w in ((pg, wg), (pu, wu)):
-            acc[rows, :] = jnp.zeros((256, 512), jnp.float32)
+    for a in both:
+        arrived(a, 0, slot(0, 0, 1, 0))
+        to_second(a, 0, 0, 1, 0)
+
+    def z_main(j):
+        for a in both:
+            arrived(a, 1, slot(0, 0, 0, far[j]))
+            chain(a, 1, 0, 0, far[j])
+            to_first(a, 1, 0, 0, far[j])
+            to_second(a, 1, 0, 0, far[j])
+            to_sib(a, 1, 0, 0, far[j])
+
+    def first_main(r):
+        for a in both:
+            arrived(a, 1, slot(0, 0, 1, r))
+            to_second(a, 1, 0, 1, r)
+            to_sib(a, 1, 0, 1, r)
+
+    def z_early(j):
+        for second, first in ((0, 0), (0, 1), (1, 0), (1, 1)):
+            for a in both:
+                arrived(a, 0, slot(second, 0, first, far[j]))
+                chain(a, 0, second, first, far[j])
+                to_sib(a, 0, second, first, far[j])
+
+    def second_main(first, r):
+        for a in both:
+            arrived(a, 1, slot(1, 0, first, r))
+            to_sib(a, 1, 1, first, r)
+
+    z_main(0)
+    for a in both:
+        chain_own(a, 0, 0, 1)
+        to_sib(a, 0, 0, 1, 0)
+    for first in (0, 1):
+        for a in both:
+            arrived(a, 0, slot(1, 0, first, 0))
+            chain_own(a, 0, 1, first)
+            to_sib(a, 0, 1, first, 0)
+    z_main(1)
+    first_main(0)
+    z_main(2)
+    z_early(0)
+    first_main(far[0])
+    z_early(1)
+    first_main(far[1])
+    first_main(far[2])
+
+    step = 1536
+
+    def forward(row, n, start, tiles, width_k):
+        rows = pl.ds(row, n)
 
         def body(k, carry):
-            cols = pl.ds(pl.multiple_of(k * step, 256), step)
+            cols = pl.ds(pl.multiple_of(start + k * width_k, 256), width_k)
             left = gx[rows, cols]
             pg[rows, :] += jnp.dot(left, wg[cols, :], preferred_element_type=jnp.float32)
             pu[rows, :] += jnp.dot(left, wu[cols, :], preferred_element_type=jnp.float32)
             return carry
 
-        lax.fori_loop(0, width // step, body, 0)
-
-    def backward(half):
-        rows = pl.ds(half * 256, 256)
-        bg[rows, :] = jnp.zeros((256, 512), jnp.float32)
+        lax.fori_loop(0, tiles, body, 0)
+
+    def backward(row, n, start, tiles, width_k):
+        rows = pl.ds(row, n)
 
         def body(k, carry):
-            cols = pl.ds(pl.multiple_of(k * step, 256), step)
+            cols = pl.ds(pl.multiple_of(start + k * width_k, 256), width_k)
             bg[rows, :] += lax.dot_general(
                 gdy[rows, cols], wd[:, cols], NT, preferred_element_type=jnp.float32
             )
             return carry
 
-        lax.fori_loop(0, width // step, body, 0)
-
+        lax.fori_loop(0, tiles, body, 0)
+
+    def clear(i, carry):
+        rows = pl.ds(pl.multiple_of(i * 64, 64), 64)
+        for acc in (pg, pu, bg):
+            acc[rows, :] = jnp.zeros((64, 512), jnp.float32)
+        return carry
+
+    lax.fori_loop(0, 8, clear, 0)
     for c in weight_copies:
         c.wait()
-    for a in (0, 1):
+    main_tiles = (width - early) // step
+    for a in both:
         for first in (0, 1):
-            for r in order:
-                arrived(a, slot(0, 1, first, r))
-        (forward, backward)[a](0)
-    for first in (0, 1):
-        for r in order:
-            for a in (0, 1):
-                arrived(a, slot(1, 0, first, r))
-                spread(a, 1, first, r)
-    for a in (0, 1):
+            for r in range(4):
+                arrived(a, 1, slot(0, 1, first, r))
+        (forward, backward)[a](0, 256, early, main_tiles, step)
+        if a == 0:
+            z_early(2)
+    for r in (0,) + far:
+        second_main(0, r)
+    for r in (0,) + far:
+        second_main(1, r)
+    for a in both:
+        for second in (0, 1):
+            for first in (0, 1):
+                for r in range(4):
+                    arrived(a, 0, slot(second, 1, first, r))
+        (forward, backward)[a](0, 512, 0, 2, early // 2)
+    for a in both:
         for first in (0, 1):
-            for r in order:
-                arrived(a, slot(1, 1, first, r))
-        (forward, backward)[a](1)
+            for r in range(4):
+                arrived(a, 1, slot(1, 1, first, r))
+        (forward, backward)[a](256, 256, early, main_tiles, step)
 
     lane = lax.broadcasted_iota(jnp.int32, (64, 128), 1)
     for dc in (1, 0):
@@ -406,7 +494,7 @@
     def launch(p, name, *copies):
         for c in copies:
             c.start()
-            sends.append(c)
+            sends.append((None, c))
         flight[p, name] = copies
 
     def landed(p, name):
@@ -498,8 +586,11 @@
                 stage(p)
     for p in range(4):
         stage_last(p)
-    for c in sends:
-        c.wait_send()
+    for cond, c in sends:
+        if cond is None:
+            c.wait_send()
+        else:
+            pl.when(cond)(c.wait_send)
 
 
 def on_device_kernel(tokens, out_grads, routes, gate_values, gate_weight, up_weight, down_weight):
@@ -545,8 +636,8 @@
             pltpu.VMEM((4, 16, total), bf16),
             pltpu.VMEM((3, 16, total), bf16),
             pltpu.SemaphoreType.DMA((6,)),
-            pltpu.SemaphoreType.DMA((2, 32)),
-            pltpu.SemaphoreType.DMA((2, 32)),
+            pltpu.SemaphoreType.DMA((4, 40)),
+            pltpu.SemaphoreType.DMA((4, 32)),
             pltpu.SemaphoreType.DMA((4, 8)),
             pltpu.SemaphoreType.DMA((4, 8)),
         ],

time: 162 us -> 140 us (0.86)
  Pallas kernels: 155 us -> 134 us
    pallas_call x1, Pallas kernels: 155 us -> 134 us  [on_device_kernel(): pl.pallas_call(pair_kernel, out_shape=(jax.ShapeDtypeStruct((rows, width)...]
where the time goes in v3:
time: 140 us
  Pallas kernels  134 us (96%)
  local copies, waits for them, and re-layouts  4.51 us (3%)
    pallas_call x1, Pallas kernels, on_device_kernel(): pl.pallas_call(pair_kernel, out_shape=(jax.ShapeDtypeStruct((rows, width)...  134 us
    unnamed x4, local copies, waits for them, and re-layouts  4.51 us

profile of v3, /device:TPU:0, one launch (start us, length us, event | category | flops | bytes accessed | tf_op | source)
XLA Modules:
  0.0 139.9 jit_solution(7609434616521523997)
XLA Ops:
  0.6 0.8 copy.12
  1.4 0.8 copy.13
  2.2 0.1 select_reduce_fusion.1
  2.3 0.7 fusion.7.aux
  3.0 133.9 %shard_map.86 = (bf16[16,7168]{1,0:T(8,128)(2,1)}, f32[16,128]{1,0:T(8,128)}) custom-call(bf16[16,7168]{1,0:T(8,128)(2,1)} %tok.1, bf16[16,7168]{1,0:T(8,128)(2,1)} %dyo.1, bf16[16,128]{1,0:T(8,128)(2,1)} %fusion.7.aux, bf16[7168,512]{1,0:T(8,128)(2,1)} %bitcast.5, bf16[7168,512]{1,0:T(8,128)(2,1)} %bitcast.6, bf16[512,7168]{1,0:T(8,128)(2,1)} %bitcast.7), custom_call_target="tpu_custom_call" | custom-call | flops 18790481920 | bytes 22020096 | tf_op jit(solution)/shard_map/pallas_call | solution.py:611
  136.9 1.4 copy.14
  138.3 1.6 %copy.16 = bf16[16,7168]{1,0:T(8,128)(2,1)} copy(bf16[16,7168]{1,0:T(8,128)(2,1)} %get-tuple-element.17) | data formatting | bytes 458752
  (2 shorter events, 0.0 us)

commit v4 on v3

--- a/solution.py
+++ b/solution.py
@@ -405,14 +405,14 @@
             z_early(2)
     for r in (0,) + far:
         second_main(0, r)
-    for r in (0,) + far:
-        second_main(1, r)
     for a in both:
         for second in (0, 1):
             for first in (0, 1):
                 for r in range(4):
                     arrived(a, 0, slot(second, 1, first, r))
         (forward, backward)[a](0, 512, 0, 2, early // 2)
+    for r in (0,) + far:
+        second_main(1, r)
     for a in both:
         for first in (0, 1):
             for r in range(4):
@@ -420,6 +420,8 @@
         (forward, backward)[a](256, 256, early, main_tiles, step)
 
     lane = lax.broadcasted_iota(jnp.int32, (64, 128), 1)
+    lane3 = lax.broadcasted_iota(jnp.int32, (4, 16, 128), 2)
+    row = lax.broadcasted_iota(jnp.int32, (4, 16, 128), 1)
     for dc in (1, 0):
         for dy in (0, 1):
             for dx in (0, 1):
@@ -427,12 +429,14 @@
                 at_dy = pl.ds((dx * 4 + dc * 2 + dy) * 64, 64)
                 group = dc * 4 + dy * 2 + dx
                 at = pl.ds(group * 64, 64)
-                info = gx[at_x, pl.ds(width, 128)].astype(jnp.float32)
-                hot = (lane % 16 == expert) & (lane < 48)
-                weight = jnp.sum(jnp.where(hot, info, 0.0), axis=1, keepdims=True)
+                info = gx[at_x, pl.ds(width, 128)].astype(jnp.float32).reshape(4, 16, 128)
+                info = jnp.sum(jnp.where(row == expert, info, 0.0), axis=1, keepdims=True)
+                info = jnp.broadcast_to(info, (4, 16, 128))
+                own = (lane3 % 16 == row) & (lane3 < 48)
+                weight = jnp.sum(jnp.where(own, info, 0.0), axis=2, keepdims=True).reshape(64, 1)
                 pick = jnp.sum(
-                    jnp.where(lane == 48 + expert, info, 0.0), axis=1, keepdims=True
-                )
+                    jnp.where(lane3 == 48 + row, info, 0.0), axis=2, keepdims=True
+                ).reshape(64, 1)
                 pre_gate = pg[at_x, :]
                 pre_up = pu[at_x, :]
                 back = bg[at_dy, :]
@@ -456,6 +460,14 @@
     quarter = width // 4
     pieces = [pl.ds(p * quarter, quarter + (256 if p == 3 else 0)) for p in range(4)]
 
+    halves = [
+        (
+            pl.ds(p * quarter, quarter // 2),
+            pl.ds(p * quarter + quarter // 2, quarter // 2 + (256 if p == 3 else 0)),
+        )
+        for p in range(4)
+    ]
+
     def product(dc, p):
         rows = pl.ds(dc * 256, 256)
 
@@ -525,26 +537,27 @@
                 return carry
 
             lax.fori_loop(0, 16, body, 0)
-        if p % 2 == 0:
-            launch(p, 1, rs_copy(p, 1, part.at[pl.ds(8, 8), :, cols], from_one.at[:, :, cols], y_nbr))
-        else:
-            launch(
-                p,
-                1,
-                rs_copy(p, 1, part.at[pl.ds(4, 4), :, cols], from_one.at[pl.ds(0, 4), :, cols], x_nbr),
-                rs_copy(p, 2, part.at[pl.ds(12, 4), :, cols], from_one.at[pl.ds(4, 4), :, cols], x_nbr),
-            )
+        a_cols, b_cols = halves[p]
+        launch(
+            p,
+            1,
+            rs_copy(p, 1, part.at[pl.ds(8, 8), :, a_cols], from_one.at[:, :, a_cols], y_nbr),
+            rs_copy(p, 2, part.at[pl.ds(4, 4), :, b_cols], from_one.at[pl.ds(0, 4), :, b_cols], x_nbr),
+            rs_copy(p, 3, part.at[pl.ds(12, 4), :, b_cols], from_one.at[pl.ds(4, 4), :, b_cols], x_nbr),
+        )
 
     def stage_two(p):
-        cols = pieces[p]
+        a_cols, b_cols = halves[p]
         landed(p, 1)
-        if p % 2 == 0:
-            add(0, from_one, 0, 8, cols)
-            launch(p, 2, rs_copy(p, 3, part.at[pl.ds(4, 4), :, cols], from_two.at[:, :, cols], x_nbr))
-        else:
-            add(0, from_one, 0, 4, cols)
-            add(8, from_one, 4, 4, cols)
-            launch(p, 2, rs_copy(p, 3, part.at[pl.ds(8, 4), :, cols], from_two.at[:, :, cols], y_nbr))
+        add(0, from_one, 0, 8, a_cols)
+        add(0, from_one, 0, 4, b_cols)
+        add(8, from_one, 4, 4, b_cols)
+        launch(
+            p,
+            2,
+            rs_copy(p, 4, part.at[pl.ds(4, 4), :, a_cols], from_two.at[:, :, a_cols], x_nbr),
+            rs_copy(p, 5, part.at[pl.ds(8, 4), :, b_cols], from_two.at[:, :, b_cols], y_nbr),
+        )
 
     def stage_three(p):
         cols = pieces[p]
@@ -554,7 +567,7 @@
             p,
             3,
             *[
-                rs_copy(p, 3 + r, part.at[r, :, cols], from_z.at[r - 1, :, cols], z_peer[r])
+                rs_copy(p, 5 + r, part.at[r, :, cols], from_z.at[r - 1, :, cols], z_peer[r])
                 for r in (2, 1, 3)
             ],
         )
@@ -573,18 +586,24 @@
         cols = pl.ds(p * quarter, quarter)
         dx_out[:, cols] = total(cols).astype(jnp.bfloat16)
         if p == 3:
-            gate_out[...] = total(pl.ds(width, 128)) + total(pl.ds(width + 128, 128))
+            gates = total(pl.ds(width, 128)) + total(pl.ds(width + 128, 128))
+            gate_out[...] = gates.T[: gate_out.shape[0], :]
 
     for p in range(4):
         product(1, p)
         stage_sib(p)
         product(0, p)
         stage_one(p)
-    for pair in ((0, 1), (2, 3)):
-        for stage in (stage_two, stage_three):
-            for p in pair:
-                stage(p)
-    for p in range(4):
+        if p >= 2:
+            stage_two(p - 2)
+    stage_three(0)
+    stage_two(2)
+    stage_three(1)
+    stage_two(3)
+    stage_three(2)
+    stage_last(0)
+    stage_three(3)
+    for p in (1, 2, 3):
         stage_last(p)
     for cond, c in sends:
         if cond is None:
@@ -596,15 +615,17 @@
 def on_device_kernel(tokens, out_grads, routes, gate_values, gate_weight, up_weight, down_weight):
     rows, width = tokens.shape
     experts = lax.axis_size("node") * lax.axis_size("local") // 2
-    hot = routes[:, :, None] == jnp.arange(experts, dtype=jnp.int32)[None, None, :]
-    table = jnp.sum(jnp.where(hot, gate_values[:, :, None], 0.0), axis=1)
+    picks = routes.shape[1]
+    expert_ids = jnp.arange(experts, dtype=jnp.int32)[:, None, None]
+    hot = routes.T[None, :, :] == expert_ids
+    table = jnp.sum(jnp.where(hot, gate_values.T[None, :, :], 0.0), axis=1)
     high = lax.reduce_precision(table, 8, 7)
     mid = lax.reduce_precision(table - high, 8, 7)
     low = table - high - mid
-    picks = jnp.arange(1, routes.shape[1] + 1, dtype=jnp.float32)[None, :, None]
-    pick = jnp.sum(jnp.where(hot, picks, 0.0), axis=1)
+    numbers = jnp.arange(1, picks + 1, dtype=jnp.float32)[None, :, None]
+    pick = jnp.sum(jnp.where(hot, numbers, 0.0), axis=1)
     aux = jnp.concatenate([high, mid, low, pick], axis=1)
-    aux = jnp.pad(aux, ((0, 0), (0, 128 - 4 * experts))).astype(jnp.bfloat16)
+    aux = jnp.pad(aux, ((0, 0), (0, 128 - 4 * rows))).astype(jnp.bfloat16)
     half = gate_weight.shape[2]
     total = width + 256
     bf16, f32 = jnp.bfloat16, jnp.float32
@@ -612,7 +633,7 @@
         pair_kernel,
         out_shape=(
             jax.ShapeDtypeStruct((rows, width), bf16),
-            jax.ShapeDtypeStruct((rows, 128), f32),
+            jax.ShapeDtypeStruct((picks, rows), f32),
         ),
         in_specs=[pl.BlockSpec(memory_space=pl.ANY)] * 6,
         out_specs=(
@@ -638,8 +659,8 @@
             pltpu.SemaphoreType.DMA((6,)),
             pltpu.SemaphoreType.DMA((4, 40)),
             pltpu.SemaphoreType.DMA((4, 32)),
-            pltpu.SemaphoreType.DMA((4, 8)),
-            pltpu.SemaphoreType.DMA((4, 8)),
+            pltpu.SemaphoreType.DMA((4, 9)),
+            pltpu.SemaphoreType.DMA((4, 9)),
         ],
         compiler_params=pltpu.CompilerParams(
             collective_id=0, has_side_effects=True, vmem_limit_bytes=62 * 1024 * 1024
@@ -648,7 +669,7 @@
             flops=10 * 512 * width * half, bytes_accessed=6 * width * half, transcendentals=0
         ),
     )(tokens, out_grads, aux, gate_weight[0], up_weight[0], down_weight[0])
-    return dx, gate[:, : routes.shape[1]]
+    return dx, gate.T
 
 
 def solution(mesh):

time: 140 us -> 129 us (0.921)
  Pallas kernels: 134 us -> 124 us
  local copies, waits for them, and re-layouts: 4.51 us -> 2.91 us
    pallas_call x1, Pallas kernels: 134 us -> 124 us  [on_device_kernel(): pl.pallas_call(pair_kernel, out_shape=(jax.ShapeDtypeStruct((rows, width)...]
    unnamed x4 -> x2, local copies, waits for them, and re-layouts: 4.51 us -> 2.91 us
where the time goes in v4:
time: 129 us
  Pallas kernels  124 us (96%)
  local copies, waits for them, and re-layouts  2.91 us (2%)
  other arithmetic  1.49 us (1%)
    pallas_call x1, Pallas kernels, on_device_kernel(): pl.pallas_call(pair_kernel, out_shape=(jax.ShapeDtypeStruct((rows, width)...  124 us
    unnamed x2, local copies, waits for them, and re-layouts  2.91 us

profile of v4, /device:TPU:0, one launch (start us, length us, event | category | flops | bytes accessed | tf_op | source)
XLA Modules:
  0.0 128.8 jit_solution(17167394167205015752)
XLA Ops:
  0.6 0.8 select_reduce_fusion.1
  1.5 0.7 fusion.7.aux
  2.1 123.7 %shard_map.86 = (bf16[16,7168]{1,0:T(8,128)(2,1)}, f32[8,16]{1,0:T(8,128)}) custom-call(bf16[16,7168]{1,0:T(8,128)(2,1)} %tok.1, bf16[16,7168]{1,0:T(8,128)(2,1)} %dyo.1, bf16[16,128]{1,0:T(8,128)(2,1)} %fusion.7.aux, bf16[7168,512]{1,0:T(8,128)(2,1)} %bitcast.9, bf16[7168,512]{1,0:T(8,128)(2,1)} %bitcast.10, bf16[512,7168]{1,0:T(8,128)(2,1)} %bitcast.11), custom_call_target="tpu_custom_call" | custom-call | flops 18790481920 | bytes 22020096 | tf_op jit(solution)/shard_map/pallas_call | solution.py:632
  125.9 1.6 %copy.11 = bf16[16,7168]{1,0:T(8,128)(2,1)} copy(bf16[16,7168]{1,0:T(8,128)(2,1)} %get-tuple-element.13) | data formatting | bytes 458752
  127.5 1.3 copy.12
  (2 shorter events, 0.0 us)

commit v5 on v4

--- a/solution.py
+++ b/solution.py
@@ -227,12 +227,12 @@
     buffers = (gx, gdy)
     first_nbr = (x_nbr, y_nbr)
     second_nbr = (y_nbr, x_nbr)
-    early = 1024
+    early = 1536
     sends = []
     counts = [0, 0, 0, 0]
 
     def slot(second, dc, first, r):
-        return second * 16 + dc * 8 + first * 4 + r
+        return second * 16 + first * 8 + dc * 4 + r
 
     def block(a, e, s):
         whole = buffers[a].shape[1]
@@ -360,7 +360,7 @@
     first_main(far[1])
     first_main(far[2])
 
-    step = 1536
+    step = (width - early) // 2
 
     def forward(row, n, start, tiles, width_k):
         rows = pl.ds(row, n)
@@ -403,21 +403,26 @@
         (forward, backward)[a](0, 256, early, main_tiles, step)
         if a == 0:
             z_early(2)
+    def second_products(first):
+        for a in both:
+            for r in range(4):
+                arrived(a, 1, slot(1, 1, first, r))
+            (forward, backward)[a](256 + first * 128, 128, early, main_tiles, step)
+
     for r in (0,) + far:
         second_main(0, r)
+    second_products(0)
+    second_main(1, 0)
+    second_main(1, far[0])
     for a in both:
         for second in (0, 1):
             for first in (0, 1):
                 for r in range(4):
                     arrived(a, 0, slot(second, 1, first, r))
         (forward, backward)[a](0, 512, 0, 2, early // 2)
-    for r in (0,) + far:
-        second_main(1, r)
-    for a in both:
-        for first in (0, 1):
-            for r in range(4):
-                arrived(a, 1, slot(1, 1, first, r))
-        (forward, backward)[a](256, 256, early, main_tiles, step)
+    second_main(1, far[1])
+    second_main(1, far[2])
+    second_products(1)
 
     lane = lax.broadcasted_iota(jnp.int32, (64, 128), 1)
     lane3 = lax.broadcasted_iota(jnp.int32, (4, 16, 128), 2)
@@ -425,8 +430,8 @@
     for dc in (1, 0):
         for dy in (0, 1):
             for dx in (0, 1):
-                at_x = pl.ds((dy * 4 + dc * 2 + dx) * 64, 64)
-                at_dy = pl.ds((dx * 4 + dc * 2 + dy) * 64, 64)
+                at_x = pl.ds((dy * 4 + dx * 2 + dc) * 64, 64)
+                at_dy = pl.ds((dx * 4 + dy * 2 + dc) * 64, 64)
                 group = dc * 4 + dy * 2 + dx
                 at = pl.ds(group * 64, 64)
                 info = gx[at_x, pl.ds(width, 128)].astype(jnp.float32).reshape(4, 16, 128)
@@ -457,29 +462,31 @@
                 part[blocks, :, pl.ds(width, 128)] = high.reshape(4, 16, 128)
                 part[blocks, :, pl.ds(width + 128, 128)] = low.reshape(4, 16, 128)
 
-    quarter = width // 4
-    pieces = [pl.ds(p * quarter, quarter + (256 if p == 3 else 0)) for p in range(4)]
-
+    sizes = (1024, 1792, 1792, 1536, width - 6144)
+    last = len(sizes) - 1
+    starts = [sum(sizes[:p]) for p in range(last + 1)]
+    tails = [256 if p == last else 0 for p in range(last + 1)]
+    pieces = [pl.ds(starts[p], sizes[p] + tails[p]) for p in range(last + 1)]
     halves = [
         (
-            pl.ds(p * quarter, quarter // 2),
-            pl.ds(p * quarter + quarter // 2, quarter // 2 + (256 if p == 3 else 0)),
+            pl.ds(starts[p], sizes[p] // 2),
+            pl.ds(starts[p] + sizes[p] // 2, sizes[p] // 2 + tails[p]),
         )
-        for p in range(4)
+        for p in range(last + 1)
     ]
 
     def product(dc, p):
         rows = pl.ds(dc * 256, 256)
 
         def body(n, carry):
-            cols = pl.ds(pl.multiple_of(p * quarter + n * 256, 256), 256)
+            cols = pl.ds(pl.multiple_of(starts[p] + n * 256, 256), 256)
             out = lax.dot_general(
                 dg[rows, :], wg[cols, :], NT, preferred_element_type=jnp.float32
             ) + lax.dot_general(du[rows, :], wu[cols, :], NT, preferred_element_type=jnp.float32)
             part[pl.ds(dc * 16, 16), :, cols] = out.astype(jnp.bfloat16).reshape(16, 16, 256)
             return carry
 
-        lax.fori_loop(0, quarter // 256, body, 0)
+        lax.fori_loop(0, sizes[p] // 256, body, 0)
 
     def rs_copy(p, lane_at, src, dst, dev):
         return pltpu.make_async_remote_copy(
@@ -520,8 +527,8 @@
     def stage_one(p):
         cols = pieces[p]
         landed(p, 0)
-        add(0, from_sib, 0, 16, pl.ds(p * quarter, quarter))
-        if p == 3:
+        add(0, from_sib, 0, 16, pl.ds(starts[p], sizes[p]))
+        if p == last:
             hi, lo = pl.ds(width, 128), pl.ds(width + 128, 128)
 
             def body(i, carry):
@@ -583,28 +590,29 @@
                 + from_z[2, :, cols].astype(jnp.float32)
             )
 
-        cols = pl.ds(p * quarter, quarter)
+        cols = pl.ds(starts[p], sizes[p])
         dx_out[:, cols] = total(cols).astype(jnp.bfloat16)
-        if p == 3:
+        if p == last:
             gates = total(pl.ds(width, 128)) + total(pl.ds(width + 128, 128))
             gate_out[...] = gates.T[: gate_out.shape[0], :]
 
-    for p in range(4):
+    for p in range(last + 1):
         product(1, p)
         stage_sib(p)
         product(0, p)
         stage_one(p)
         if p >= 2:
             stage_two(p - 2)
-    stage_three(0)
-    stage_two(2)
-    stage_three(1)
-    stage_two(3)
-    stage_three(2)
-    stage_last(0)
-    stage_three(3)
-    for p in (1, 2, 3):
-        stage_last(p)
+        if p >= 4:
+            stage_three(p - 4)
+    for p in range(last - 1, last + 1):
+        stage_two(p)
+        stage_three(p - 2)
+        stage_last(p - 3)
+    for p in range(last - 1, last + 1):
+        stage_three(p)
+        stage_last(p - 1)
+    stage_last(last)
     for cond, c in sends:
         if cond is None:
             c.wait_send()
@@ -659,8 +667,8 @@
             pltpu.SemaphoreType.DMA((6,)),
             pltpu.SemaphoreType.DMA((4, 40)),
             pltpu.SemaphoreType.DMA((4, 32)),
-            pltpu.SemaphoreType.DMA((4, 9)),
-            pltpu.SemaphoreType.DMA((4, 9)),
+            pltpu.SemaphoreType.DMA((5, 9)),
+            pltpu.SemaphoreType.DMA((5, 9)),
         ],
         compiler_params=pltpu.CompilerParams(
             collective_id=0, has_side_effects=True, vmem_limit_bytes=62 * 1024 * 1024

time: 129 us -> 133 us (1.031)
  Pallas kernels: 124 us -> 128 us
    pallas_call x1, Pallas kernels: 124 us -> 128 us  [on_device_kernel(): pl.pallas_call(pair_kernel, out_shape=(jax.ShapeDtypeStruct((rows, width)...]
where the time goes in v5:
time: 133 us
  Pallas kernels  128 us (96%)
  local copies, waits for them, and re-layouts  2.91 us (2%)
  other arithmetic  1.49 us (1%)
    pallas_call x1, Pallas kernels, on_device_kernel(): pl.pallas_call(pair_kernel, out_shape=(jax.ShapeDtypeStruct((rows, width)...  128 us
    unnamed x2, local copies, waits for them, and re-layouts  2.91 us

profile of v5, /device:TPU:0, one launch (start us, length us, event | category | flops | bytes accessed | tf_op | source)
XLA Modules:
  0.0 133.0 jit_solution(7538867698182846227)
XLA Ops:
  0.6 0.8 select_reduce_fusion.1
  1.5 0.7 fusion.7.aux
  2.1 128.0 %shard_map.86 = (bf16[16,7168]{1,0:T(8,128)(2,1)}, f32[8,16]{1,0:T(8,128)}) custom-call(bf16[16,7168]{1,0:T(8,128)(2,1)} %tok.1, bf16[16,7168]{1,0:T(8,128)(2,1)} %dyo.1, bf16[16,128]{1,0:T(8,128)(2,1)} %fusion.7.aux, bf16[7168,512]{1,0:T(8,128)(2,1)} %bitcast.9, bf16[7168,512]{1,0:T(8,128)(2,1)} %bitcast.10, bf16[512,7168]{1,0:T(8,128)(2,1)} %bitcast.11), custom_call_target="tpu_custom_call" | custom-call | flops 18790481920 | bytes 22020096 | tf_op jit(solution)/shard_map/pallas_call | solution.py:640
  130.1 1.6 %copy.11 = bf16[16,7168]{1,0:T(8,128)(2,1)} copy(bf16[16,7168]{1,0:T(8,128)(2,1)} %get-tuple-element.13) | data formatting | bytes 458752
  131.8 1.3 copy.12
  (2 shorter events, 0.0 us)
